TPU v7x, 256 devices: a whole 4x4x8 slice. The times are simulated.
256 devices in a mesh: freq: 4 (over y_hi, core), space: 64 (over x, y_lo, z).
Axes of the slice: x: 4, y: 4 (y_hi: 2, y_lo: 2; y = y_hi * 2 + y_lo), z: 8, core: 2. Of those that a mesh axis runs over, the one named last changes fastest.
Arguments:
- reflection: float32 [2, 32, 1024, 1024], P(None, 'freq', 'space'), may hold values from -6 to 6
- phase: float32 [32, 1024], P('freq'), may hold values from -3.140625 to 3.140625
- group_index: int32 [32], P('freq'), may hold values from 0 to 3
- widths: int32 [64, 2], P('space'), may hold values from 1 to 16
Outputs:
- corrected: float32 [2, 4, 1024, 1024], P(None, 'freq', None, 'space')
Inputs may be any that keep to these rules, and one draw needn't show every extreme that they name: `group_index`: each frequency belongs to one depth group. `widths`: margins of a patch are at most one column block wide.
All inputs are finite; a program needn't handle non-finite values.
Results may differ from a plain program's by a relative error of at most 0.0003.
Values sent between devices are 32-bit elements; how exact they have to be, the bound alone decides.
A program may use at most 64 MiB of HBM per device.

v0:
```python
import math

import jax
import jax.numpy as jnp
from jax import lax
from jax.sharding import PartitionSpec as P

ITERS = 3


def in_blocks(array, dim, devices):
    shape = array.shape
    parts = array.reshape(*shape[:dim], devices, shape[dim] // devices, *shape[dim + 1 :])
    return jnp.moveaxis(parts, dim, 0)


def sum_at_owner(array, axis, dim):
    parts = in_blocks(array, dim, lax.axis_size(axis))
    arrived = lax.all_to_all(parts, axis, split_axis=0, concat_axis=0, tiled=True)
    return arrived.sum(axis=0)


def padded(array, sides, width):
    for axis, dim in sides:
        devices, length = (lax.axis_size(axis), array.shape[dim])
        up = [(i, (i + 1) % devices) for i in range(devices)]
        down = [(j, i) for i, j in up]
        last = lax.slice_in_dim(array, length - width, length, axis=dim)
        leading = lax.slice_in_dim(array, 0, width, axis=dim)
        before = lax.ppermute(last, axis, up)
        after = lax.ppermute(leading, axis, down)
        array = jnp.concatenate([before, array, after], axis=dim)
    return array


def factor_tables(length):
    first = 1
    for divisor in range(1, math.isqrt(length) + 1):
        if length % divisor == 0:
            first = divisor
    second = length // first
    scale = 1.0 / math.sqrt(length)
    outer_a = jnp.arange(first, dtype=jnp.int32)
    outer_b = jnp.arange(second, dtype=jnp.int32)
    angle_a = (outer_a[:, None] * outer_a[None, :] % first).astype(jnp.float32) * (
        -2.0 * math.pi / first
    )
    angle_t = (outer_a[:, None] * outer_b[None, :] % length).astype(jnp.float32) * (
        -2.0 * math.pi / length
    )
    angle_b = (outer_b[:, None] * outer_b[None, :] % second).astype(jnp.float32) * (
        -2.0 * math.pi / second
    )
    return (
        jnp.cos(angle_a) * scale,
        jnp.sin(angle_a) * scale,
        jnp.cos(angle_t),
        jnp.sin(angle_t),
        jnp.cos(angle_b),
        jnp.sin(angle_b),
    )


def hmul(left, right):
    return jnp.matmul(
        left, right, precision=lax.Precision.HIGHEST, preferred_element_type=jnp.float32
    )


def heinsum(form, left, right):
    return jnp.einsum(
        form, left, right, precision=lax.Precision.HIGHEST, preferred_element_type=jnp.float32
    )


def complex_mix(form, real_part, imag_part, table_r, table_i):
    out_r = heinsum(form, real_part, table_r) - heinsum(form, imag_part, table_i)
    out_i = heinsum(form, real_part, table_i) + heinsum(form, imag_part, table_r)
    return (out_r, out_i)


def columns_transform(real_part, imag_part, tables):
    first_r, first_i, twist_r, twist_i, second_r, second_i = tables
    shape = real_part.shape
    first = first_r.shape[0]
    second = second_r.shape[0]
    split_r = real_part.reshape(shape[:-1] + (first, second))
    split_i = imag_part.reshape(shape[:-1] + (first, second))
    mid_r, mid_i = complex_mix("...ab,ak->...kb", split_r, split_i, first_r, first_i)
    turn_r = mid_r * twist_r - mid_i * twist_i
    turn_i = mid_r * twist_i + mid_i * twist_r
    out_r, out_i = complex_mix("...kb,bm->...mk", turn_r, turn_i, second_r, second_i)
    return (out_r.reshape(shape), out_i.reshape(shape))


def rows_transform(real_part, imag_part, tables):
    first_r, first_i, twist_r, twist_i, second_r, second_i = tables
    shape = real_part.shape
    first = first_r.shape[0]
    second = second_r.shape[0]
    split_r = real_part.reshape((first, second) + shape[1:])
    split_i = imag_part.reshape((first, second) + shape[1:])
    mid_r, mid_i = complex_mix("abc,ak->kbc", split_r, split_i, first_r, first_i)
    turn_r = mid_r * twist_r[:, :, None] - mid_i * twist_i[:, :, None]
    turn_i = mid_r * twist_i[:, :, None] + mid_i * twist_r[:, :, None]
    out_r, out_i = complex_mix("kbc,bm->mkc", turn_r, turn_i, second_r, second_i)
    return (out_r.reshape(shape), out_i.reshape(shape))


def normalize(real_part, imag_part):
    power = real_part * real_part + imag_part * imag_part
    scale = 1.0 / jnp.sqrt(power + jnp.mean(power) + 1e-06)
    return (real_part * scale, imag_part * scale)


def local(reflection, phase, group_index, widths):
    width = reflection.shape[3]
    count = lax.axis_size("freq")
    spaces = lax.axis_size("space")
    block = width // spaces
    rows_here = reflection.shape[2]
    cosine = jnp.cos(phase)[:, None, :]
    sine = jnp.sin(phase)[:, None, :]
    turned_r = reflection[0] * cosine - reflection[1] * sine
    turned_i = reflection[0] * sine + reflection[1] * cosine
    onehot = (group_index[:, None] == jnp.arange(count, dtype=jnp.int32)[None, :]).astype(
        jnp.float32
    )
    partial_r = jnp.einsum("fg,frn->grn", onehot, turned_r, precision=lax.Precision.HIGHEST)
    partial_i = jnp.einsum("fg,frn->grn", onehot, turned_i, precision=lax.Precision.HIGHEST)
    tables = factor_tables(width)
    summed = sum_at_owner(jnp.stack([partial_r, partial_i], axis=1), "freq", 0)
    focus_r = summed[0, 0]
    focus_i = summed[0, 1]
    focus_r, focus_i = columns_transform(focus_r, focus_i, tables)
    blocks = jnp.stack([focus_r, focus_i]).reshape(2, rows_here, spaces, block)
    received = lax.all_to_all(blocks, "space", split_axis=2, concat_axis=1, tiled=True)
    piece_r = received[0, :, 0, :]
    piece_i = received[1, :, 0, :]
    out_r, out_i = rows_transform(piece_r, piece_i, tables)
    owned = jnp.stack([out_r, out_i])
    patch = padded(owned, (("space", 2),), block)
    position = jnp.arange(block, dtype=jnp.int32)
    left_keep = (position >= block - widths[0, 0]).astype(jnp.float32)
    right_keep = (position < widths[0, 1]).astype(jnp.float32)
    keep = jnp.concatenate([left_keep, jnp.ones((block,), jnp.float32), right_keep])
    patch_r = patch[0] * keep[None, :]
    patch_i = patch[1] * keep[None, :]
    vector_r, vector_i = normalize(jnp.sum(patch_r, axis=1), jnp.sum(patch_i, axis=1))
    for step in range(ITERS):
        back_r = hmul(vector_r, patch_r) + hmul(vector_i, patch_i)
        back_i = hmul(vector_i, patch_r) - hmul(vector_r, patch_i)
        next_r = hmul(patch_r, back_r) - hmul(patch_i, back_i)
        next_i = hmul(patch_r, back_i) + hmul(patch_i, back_r)
        vector_r, vector_i = normalize(next_r, next_i)
    own_r = patch[0][:, block : 2 * block]
    own_i = patch[1][:, block : 2 * block]
    fixed_r = vector_r[:, None] * own_r + vector_i[:, None] * own_i
    fixed_i = vector_r[:, None] * own_i - vector_i[:, None] * own_r
    return jnp.stack([fixed_r, fixed_i])[:, None]


def solution(mesh):
    in_specs = (P(None, "freq", "space", None), P("freq", None), P("freq"), P("space", None))
    out_specs = P(None, "freq", None, "space")
    return jax.shard_map(local, mesh=mesh, in_specs=in_specs, out_specs=out_specs, check_vma=False)
```

profile of v0, /device:TPU:0, one launch (start us, length us, event | category | flops | bytes accessed | tf_op | source)
XLA Modules:
  0.0 84.4 jit_solution(1748867127913777168)
XLA Ops:
  0.0 0.9 %fusion.198 = (f32[8,1024]{1,0:T(8,128)S(1)}, f32[8,1024]{1,0:T(8,128)S(1)}) fusion(f32[8,1024]{1,0:T(8,128)} %param.5), kind=kLoop, calls=%fused_computation.240 | loop fusion | bytes 98304 | tf_op jit(solution)/shard_map/cos | solution.py:122
  0.9 1.3 %fusion.14 = (f32[8,16,1024]{2,1,0:T(8,128)S(1)}, f32[8,16,1024]{2,1,0:T(8,128)S(1)}) fusion(f32[2,8,16,1024]{3,2,1,0:T(8,128)} %param.4, f32[8,1024]{1,0:T(8,128)S(1)} %get-tuple-element.27, f32[8,1024]{1,0:T(8,128)S(1)} %get-tuple-element.26), kind=kLoop, calls=%fused_computation.40 | loop fusion | flops 786432 | bytes 2162688 | tf_op jit(solution)/shard_map/sub | solution.py:124
  2.2 0.6 copy-done.1
  2.9 0.7 convolution_bitcast_fusion
  3.5 0.7 convolution_bitcast_fusion.1
  4.3 1.1 %copy.35 = f32[4,1,2,16,1024]{4,3,2,1,0:T(8,128)} copy(f32[4,1,2,16,1024]{4,0,3,2,1:T(4,128)S(1)} %maximum_bitcast_fusion) | data formatting | bytes 1048576 | tf_op jit(solution)/shard_map/reshape | solution.py:13
  5.4 3.5 %all-to-all-start = ((f32[4,1,2,16,1024]{4,3,2,1,0:T(8,128)}), f32[4,1,2,16,1024]{4,3,2,1,0:T(8,128)S(1)}, u32[]{:S(2)}, u32[]{:S(2)}) async-start(f32[4,1,2,16,1024]{4,3,2,1,0:T(8,128)} %copy.35), calls=%async_computation | async-start | bytes 1048576 | tf_op jit(solution)/shard_map/all_to_all | solution.py:19
  9.2 10.0 %all-to-all-done = f32[4,1,2,16,1024]{4,3,2,1,0:T(8,128)S(1)} async-done(((f32[4,1,2,16,1024]{4,3,2,1,0:T(8,128)}), f32[4,1,2,16,1024]{4,3,2,1,0:T(8,128)S(1)}, u32[]{:S(2)}, u32[]{:S(2)}) %all-to-all-start) | async-done | bytes 524320 | tf_op jit(solution)/shard_map/all_to_all | solution.py:19
  19.4 0.4 fusion.44
  19.8 0.4 fusion.37
  20.4 0.4 convolution_subtract_fusion.3
  20.9 0.4 convolution_add_fusion.3
  21.3 1.3 %fusion.22 = f32[32,16,32]{2,0,1:T(8,128)S(1)} fusion(f32[32,16,32]{2,0,1:T(8,128)S(1)} %convolution_add_fusion.3, f32[32,16,32]{2,0,1:T(8,128)S(1)} %convolution_subtract_fusion.3, f32[32,32]{1,0:T(8,128)S(1)} %copy.37, f32[32,32]{1,0:T(8,128)S(1)} %copy.36), kind=kOutput, calls=%fused_computation.51 | convolution fusion | flops 6354944 | bytes 204800 | tf_op jit(solution)/shard_map/...kb,bm->...mk/dot_general | solution.py:71
  22.6 1.3 %fusion.20 = f32[32,16,32]{2,0,1:T(8,128)S(1)} fusion(f32[32,16,32]{2,0,1:T(8,128)S(1)} %convolution_add_fusion.3, f32[32,16,32]{2,0,1:T(8,128)S(1)} %convolution_subtract_fusion.3, f32[32,32]{1,0:T(8,128)S(1)} %copy.37, f32[32,32]{1,0:T(8,128)S(1)} %copy.36), kind=kOutput, calls=%fused_computation.49 | convolution fusion | flops 6354944 | bytes 204800 | tf_op jit(solution)/shard_map/...kb,bm->...mk/dot_general | solution.py:71
  23.9 1.3 %fusion.1 = f32[16,32,32]{2,1,0:T(8,128)S(1)} fusion(f32[32,16,32]{2,0,1:T(8,128)S(1)} %fusion.22, f32[32,16,32]{2,0,1:T(8,128)S(1)} %convolution_add_fusion.3, f32[32,16,32]{2,0,1:T(8,128)S(1)} %convolution_subtract_fusion.3, f32[32,32]{1,0:T(8,128)S(1)} %copy.37, f32[32,32]{1,0:T(8,128)S(1)} %copy.36), kind=kOutput, calls=%fused_computation.7 | convolution fusion | flops 6371328 | bytes 270336 | tf_op jit(solution)/shard_map/...kb,bm->...mk/dot_general | solution.py:71
  25.5 1.3 %fusion = f32[16,32,32]{2,1,0:T(8,128)S(1)} fusion(f32[32,16,32]{2,0,1:T(8,128)S(1)} %fusion.20, f32[32,16,32]{2,0,1:T(8,128)S(1)} %convolution_add_fusion.3, f32[32,16,32]{2,0,1:T(8,128)S(1)} %convolution_subtract_fusion.3, f32[32,32]{1,0:T(8,128)S(1)} %copy.37, f32[32,32]{1,0:T(8,128)S(1)} %copy.36), kind=kOutput, calls=%fused_computation.5 | convolution fusion | flops 6371328 | bytes 270336 | tf_op jit(solution)/shard_map/...kb,bm->...mk/dot_general | solution.py:71
  27.0 0.6 copy.50
  27.7 1.0 %reshape.147 = f32[64,1,512]{2,1,0:T(1,128)} reshape(f32[64,2,16,16]{3,2,1,0:T(8,128)S(1)} %bitcast.260) | data formatting | bytes 262144
  28.7 11.6 %all-to-all-start.1 = ((f32[64,1,512]{2,1,0:T(1,128)}), f32[64,1,512]{2,1,0:T(1,128)S(1)}, u32[]{:S(2)}, u32[]{:S(2)}) async-start(f32[64,1,512]{2,1,0:T(1,128)} %reshape.147), calls=%async_computation.1 | async-start | bytes 262144 | tf_op jit(solution)/shard_map/all_to_all | solution.py:137
  40.4 0.6 fusion.199
  41.5 9.8 %all-to-all-done.1 = f32[64,1,512]{2,1,0:T(1,128)S(1)} async-done(((f32[64,1,512]{2,1,0:T(1,128)}), f32[64,1,512]{2,1,0:T(1,128)S(1)}, u32[]{:S(2)}, u32[]{:S(2)}) %all-to-all-start.1) | async-done | bytes 131104 | tf_op jit(solution)/shard_map/all_to_all | solution.py:137
  51.4 0.5 broadcast.291
  51.9 0.9 %reduce.1 = f32[64,512]{1,0:T(8,128)S(1)} reduce(f32[64,1,512]{2,1,0:T(1,128)S(1)} %all-to-all-done.1, f32[]{:T(128)} %broadcast.291), dimensions={1}, to_apply=%all_to_all.15.reduce_sub_computation | reduce | bytes 262148 | tf_op jit(solution)/shard_map/all_to_all | solution.py:137
  52.8 0.4 reshape.148
  53.6 0.4 fusion.41
  54.1 0.4 fusion.34
  54.8 0.4 convolution_subtract_fusion.1
  55.3 0.4 convolution_add_fusion.1
  55.7 1.3 %fusion.24 = f32[32,32,16]{1,0,2:T(8,128)S(1)} fusion(f32[32,32,16]{1,0,2:T(8,128)S(1)} %convolution_add_fusion.1, f32[32,32,16]{1,0,2:T(8,128)S(1)} %convolution_subtract_fusion.1, f32[32,32]{1,0:T(8,128)S(1)} %copy.37, f32[32,32]{1,0:T(8,128)S(1)} %copy.36), kind=kOutput, calls=%fused_computation.62 | convolution fusion | flops 6354944 | bytes 204800 | tf_op jit(solution)/shard_map/kbc,bm->mkc/dot_general | solution.py:71
  57.0 1.3 %fusion.25 = f32[32,32,16]{1,0,2:T(8,128)S(1)} fusion(f32[32,32,16]{1,0,2:T(8,128)S(1)} %convolution_add_fusion.1, f32[32,32,16]{1,0,2:T(8,128)S(1)} %convolution_subtract_fusion.1, f32[32,32]{1,0:T(8,128)S(1)} %copy.37, f32[32,32]{1,0:T(8,128)S(1)} %copy.36), kind=kOutput, calls=%fused_computation.63 | convolution fusion | flops 6354944 | bytes 204800 | tf_op jit(solution)/shard_map/kbc,bm->mkc/dot_general | solution.py:71
  58.4 1.3 %convolution_add_fusion = f32[32,32,16]{1,0,2:T(8,128)S(1)} fusion(f32[32,32,16]{1,0,2:T(8,128)S(1)} %fusion.24, f32[32,32,16]{1,0,2:T(8,128)S(1)} %convolution_add_fusion.1, f32[32,32,16]{1,0,2:T(8,128)S(1)} %convolution_subtract_fusion.1, f32[32,32]{1,0:T(8,128)S(1)} %copy.37, f32[32,32]{1,0:T(8,128)S(1)} %copy.36), kind=kOutput, calls=%fused_computation | convolution fusion | flops 6371328 | bytes 270336 | tf_op jit(solution)/shard_map/kbc,bm->mkc/dot_general | solution.py:71
  59.8 1.3 %convolution_subtract_fusion = f32[32,32,16]{1,0,2:T(8,128)S(1)} fusion(f32[32,32,16]{1,0,2:T(8,128)S(1)} %fusion.25, f32[32,32,16]{1,0,2:T(8,128)S(1)} %convolution_add_fusion.1, f32[32,32,16]{1,0,2:T(8,128)S(1)} %convolution_subtract_fusion.1, f32[32,32]{1,0:T(8,128)S(1)} %copy.37, f32[32,32]{1,0:T(8,128)S(1)} %copy.36), kind=kOutput, calls=%fused_computation.1 | convolution fusion | flops 6371328 | bytes 270336 | tf_op jit(solution)/shard_map/kbc,bm->mkc/dot_general | solution.py:71
  61.3 0.9 %collective-permute-start = (f32[2,1024,16]{1,2,0:T(8,128)S(1)}, f32[2,1024,16]{1,2,0:T(8,128)S(1)}, u32[]{:S(2)}, u32[]{:S(2)}) collective-permute-start(f32[2,1024,16]{1,2,0:T(8,128)S(1)} %constant_dynamic-update-slice_fusion), channel_id=1, source_target_pairs={{0,1},{1,2},{2,3},{3,4},{4,5},{5,6},{6,7},{7,8},{8,9},{9,10},{10,1... | collective-permute-start | bytes 393224 | tf_op jit(solution)/shard_map/ppermute | solution.py:30
  62.2 5.5 %collective-permute-start.1 = (f32[2,1024,16]{1,2,0:T(8,128)S(1)}, f32[2,1024,16]{1,2,0:T(8,128)S(1)}, u32[]{:S(2)}, u32[]{:S(2)}) collective-permute-start(f32[2,1024,16]{1,2,0:T(8,128)S(1)} %constant_dynamic-update-slice_fusion), channel_id=1, source_target_pairs={{1,0},{2,1},{3,2},{4,3},{5,4},{6,5},{7,6},{8,7},{9,8},{10,9},{11,1... | collective-permute-start | bytes 393224 | tf_op jit(solution)/shard_map/ppermute | solution.py:31
  67.7 0.6 compare_convert_fusion
  68.4 2.2 %collective-permute-done = f32[2,1024,16]{1,2,0:T(8,128)S(1)} collective-permute-done((f32[2,1024,16]{1,2,0:T(8,128)S(1)}, f32[2,1024,16]{1,2,0:T(8,128)S(1)}, u32[]{:S(2)}, u32[]{:S(2)}) %collective-permute-start) | collective-permute-done | bytes 131104 | tf_op jit(solution)/shard_map/ppermute | solution.py:30
  70.8 0.6 fusion.101
  72.0 0.3 convolution_bitcast_fusion.13
  72.3 0.3 convolution_bitcast_fusion.11
  72.7 0.3 fusion.11
  73.0 0.4 fusion.186
  73.4 0.3 fusion.194
  73.7 0.3 fusion.13
  74.0 0.3 fusion.193
  74.3 0.3 fusion.187
  74.6 0.6 fusion.102
  75.9 0.3 convolution_bitcast_fusion.9
  76.2 0.3 convolution_bitcast_fusion.7
  76.5 0.3 fusion.7
  76.9 0.4 fusion.184
  77.3 0.3 fusion.192
  77.6 0.3 fusion.9
  77.9 0.3 fusion.191
  78.2 0.3 fusion.185
  78.5 0.6 fusion.103
  80.1 0.3 convolution_bitcast_fusion.3
  80.4 0.3 fusion.3
  80.8 0.4 fusion.182
  81.1 0.3 fusion.190
  81.4 0.3 fusion.5
  81.8 0.3 fusion.189
  82.1 0.3 fusion.183
  82.4 0.6 fusion.104
  83.7 0.7 maximum_bitcast_fusion.1
  (35 shorter events, 2.6 us)
Async XLA Ops:
  2.2 0.7 copy-start.1
  5.4 13.8 %all-to-all-start = ((f32[4,1,2,16,1024]{4,3,2,1,0:T(8,128)}), f32[4,1,2,16,1024]{4,3,2,1,0:T(8,128)S(1)}, u32[]{:S(2)}, u32[]{:S(2)}) async-start(f32[4,1,2,16,1024]{4,3,2,1,0:T(8,128)} %copy.35), calls=%async_computation | async-start | bytes 1048576 | tf_op jit(solution)/shard_map/all_to_all | solution.py:19
  28.7 11.7 %copy-start = (s32[1,2]{1,0:T(1,128)S(1)}, s32[1,2]{1,0:T(1,128)}, u32[]{:S(2)}) copy-start(s32[1,2]{1,0:T(1,128)} %param.7) | copy-start | bytes 28
  28.7 22.7 %all-to-all-start.1 = ((f32[64,1,512]{2,1,0:T(1,128)}), f32[64,1,512]{2,1,0:T(1,128)S(1)}, u32[]{:S(2)}, u32[]{:S(2)}) async-start(f32[64,1,512]{2,1,0:T(1,128)} %reshape.147), calls=%async_computation.1 | async-start | bytes 262144 | tf_op jit(solution)/shard_map/all_to_all | solution.py:137
  61.3 9.3 %collective-permute-start = (f32[2,1024,16]{1,2,0:T(8,128)S(1)}, f32[2,1024,16]{1,2,0:T(8,128)S(1)}, u32[]{:S(2)}, u32[]{:S(2)}) collective-permute-start(f32[2,1024,16]{1,2,0:T(8,128)S(1)} %constant_dynamic-update-slice_fusion), channel_id=1, source_target_pairs={{0,1},{1,2},{2,3},{3,4},{4,5},{5,6},{6,7},{7,8},{8,9},{9,10},{10,1... | collective-permute-start | bytes 393224 | tf_op jit(solution)/shard_map/ppermute | solution.py:30
  62.2 8.4 %collective-permute-start.1 = (f32[2,1024,16]{1,2,0:T(8,128)S(1)}, f32[2,1024,16]{1,2,0:T(8,128)S(1)}, u32[]{:S(2)}, u32[]{:S(2)}) collective-permute-start(f32[2,1024,16]{1,2,0:T(8,128)S(1)} %constant_dynamic-update-slice_fusion), channel_id=1, source_target_pairs={{1,0},{2,1},{3,2},{4,3},{5,4},{6,5},{7,6},{8,7},{9,8},{10,9},{11,1... | collective-permute-start | bytes 393224 | tf_op jit(solution)/shard_map/ppermute | solution.py:31
where the time goes:
time: 84.7 us; the launch traced here: 84.4 us
  matrix products  23.2 us (27%)
  waiting for transfers between devices  22.1 us (26%)
  starting transfers between devices  21.4 us (25%)
  local copies, waits for them, and re-layouts  7.45 us (9%)
  other arithmetic  6.68 us (8%)
  between operations  3.58 us (4%)
    dot_general x16, matrix products, heinsum(): jnp.einsum(form, left, right, precision=lax.Precision.HIGHEST, preferred_...  14.2 us
    all_to_all x1, starting transfers between devices, local(): lax.all_to_all(blocks, 'space', split_axis=2, concat_axis=1, tiled=True)  11.6 us
    all_to_all x1, waiting for transfers between devices, sum_at_owner(): lax.all_to_all(parts, axis, split_axis=0, concat_axis=0, tiled=True)  9.99 us
    all_to_all x1, waiting for transfers between devices, local(): lax.all_to_all(blocks, 'space', split_axis=2, concat_axis=1, tiled=True)  9.84 us
    dot_general x24, matrix products, hmul(): jnp.matmul(left, right, precision=lax.Precision.HIGHEST, preferred_elemen...  7.74 us
    ppermute x1, starting transfers between devices, padded(): after = lax.ppermute(leading, axis, down)  5.47 us
    all_to_all x1, starting transfers between devices, sum_at_owner(): lax.all_to_all(parts, axis, split_axis=0, concat_axis=0, tiled=True)  3.47 us
    reduce_sum x4, other arithmetic, normalize(): scale = 1.0 / jnp.sqrt(power + jnp.mean(power) + 1e-06)  2.42 us
  transfers between devices with their start and end apart: 4, of which 3 were waited for; matrix products, arithmetic and copies ran while one was open for 2% of the time, Pallas kernels for 0%

commit v1 on v0

v1 whole, which is shorter than its diff:
```python
import functools
import math

import jax
import jax.numpy as jnp
import ml_dtypes
import numpy as np
from jax import lax
from jax.experimental import pallas as pl
from jax.experimental.pallas import tpu as pltpu
from jax.sharding import PartitionSpec as P

MESH = pl.DeviceIdType.MESH
F32 = jnp.float32
BF16 = jnp.bfloat16
ITERS = 3
N = 1024
NFD = 8
ROWS = 16
EPS = 1e-06


def split_np(table):
    hi = table.astype(np.float32).astype(ml_dtypes.bfloat16)
    lo = (table - hi.astype(np.float64)).astype(np.float32).astype(ml_dtypes.bfloat16)
    return np.stack([hi, lo])


def tables():
    lane = np.arange(128)
    k1 = np.arange(8)
    ang = 2 * np.pi * (k1[:, None] * lane[None, :] % N) / N
    twist_a = np.stack([np.cos(ang), np.sin(ang)]) / 32.0
    y_lo, x, slot, q_hi = np.meshgrid(np.arange(2), np.arange(4), np.arange(10), np.arange(2), indexing="ij")
    block = ((x * 2 + y_lo) * 8 + slot - 1) % 64
    k2 = (2 * block + q_hi).reshape(-1)
    ang = 2 * np.pi * (k2[:, None] * lane[None, :] % 128) / 128
    cos, sin = (np.cos(ang), np.sin(ang))
    real_rows = np.concatenate([cos, sin], axis=1)
    imag_rows = np.concatenate([-sin, cos], axis=1)
    col = np.stack([real_rows, imag_rows], axis=1).reshape(320, 256)
    row = np.zeros((2, 2, 2, 64, 4, 8, 2, 2, 2))
    m1 = np.arange(64)
    for mine in range(2):
        for rel in range(2):
            xs, zs = np.meshgrid(np.arange(4), np.arange(8), indexing="ij")
            s = (xs * 2 + (mine ^ rel)) * 8 + zs
            ang = 2 * np.pi * (m1[:, None, None] * s[None] % 64) / 64
            for q in range(2):
                row[mine, 0, q, :, :, :, rel, q, 0] = np.cos(ang)
                row[mine, 0, q, :, :, :, rel, q, 1] = np.sin(ang)
                row[mine, 1, q, :, :, :, rel, q, 0] = -np.sin(ang)
                row[mine, 1, q, :, :, :, rel, q, 1] = np.cos(ang)
    row = row.reshape(2, 256, 256)
    ang = 2 * np.pi * (m1[:, None] * (lane % 16)[None, :] % N) / N
    twist_b = np.stack([np.cos(ang), np.sin(ang)])
    last = np.zeros((2, 8, 16, 2, 16, 8))
    i, m2 = (np.arange(16), np.arange(16))
    ang = 2 * np.pi * (i[:, None] * m2[None, :] % 16) / 16
    for k in range(8):
        last[0, k, :, 0, :, k] = np.cos(ang)
        last[1, k, :, 0, :, k] = np.sin(ang)
        last[0, k, :, 1, :, k] = -np.sin(ang)
        last[1, k, :, 1, :, k] = np.cos(ang)
    last = last.reshape(256, 256) / 32.0
    over_k1 = (lane[:, None] // 8 == lane[None, :] // 8).astype(np.float64)
    over_m2 = (lane[:, None] % 8 == lane[None, :] % 8).astype(np.float64)
    sums = np.stack([np.concatenate([t, t], axis=0) for t in (over_k1, over_m2)]).astype(ml_dtypes.bfloat16)
    return (
        twist_a.astype(np.float32),
        split_np(col),
        np.moveaxis(split_np(row), 0, 1),
        twist_b.astype(np.float32),
        split_np(last),
        sums,
    )


def halves(value):
    hi = value.astype(BF16)
    lo = (value - hi.astype(F32)).astype(BF16)
    return (hi, lo)


def dft4(v):
    (ar, ai), (br, bi), (cr, ci), (dr, di) = v
    pr, pi, mr, mi = (ar + cr, ai + ci, ar - cr, ai - ci)
    qr, qi, nr, ni = (br + dr, bi + di, br - dr, bi - di)
    return [(pr + qr, pi + qi), (mr + ni, mi - nr), (pr - qr, pi - qi), (mr - ni, mi + nr)]


def dft8(v):
    even = dft4(v[0::2])
    odd = dft4(v[1::2])
    half = math.sqrt(0.5)
    o1r, o1i = odd[1]
    o2r, o2i = odd[2]
    o3r, o3i = odd[3]
    turned = [
        odd[0],
        ((o1r + o1i) * half, (o1i - o1r) * half),
        (o2i, -o2r),
        ((o3i - o3r) * half, -(o3r + o3i) * half),
    ]
    low = [(e[0] + t[0], e[1] + t[1]) for e, t in zip(even, turned)]
    high = [(e[0] - t[0], e[1] - t[1]) for e, t in zip(even, turned)]
    return low + high


def matmul(left, right):
    return jnp.dot(left, right, preferred_element_type=F32)


def matmul_t(left, right):
    return lax.dot_general(left, right, (((1,), (1,)), ((), ())), preferred_element_type=F32)


def wait_bytes(ref, sem):
    pltpu.make_async_copy(ref, ref, sem).wait()


def kernel(
    refl_hbm, phase_hbm, group_hbm, widths_hbm, twa_hbm, col_hbm, row_hbm, twb_hbm, last_hbm, sums_hbm,
    out_ref,
    refl, phase, group, widths, twa, col, row, twb, last, sums,
    core_out, core_own, core_in, xsplit, y_out, y_in, q_buf, r_buf, rsplit, vsplit, t_buf,
    load_sem, core_sem, y_sem, a2a_sem,
):
    f = lax.axis_index("freq")
    s = lax.axis_index("space")
    y_hi = f // 2
    core = lax.rem(f, 2)
    x = s // 16
    y_lo = lax.rem(s // 8, 2)
    z = lax.rem(s, 8)

    loads = [
        pltpu.make_async_copy(src, dst, load_sem.at[n])
        for n, (src, dst) in enumerate(
            [
                (group_hbm, group), (phase_hbm, phase), (refl_hbm, refl), (twa_hbm, twa), (col_hbm, col),
                (row_hbm.at[y_lo], row), (twb_hbm, twb), (last_hbm, last), (sums_hbm, sums), (widths_hbm, widths),
            ]
        )
    ]
    for load in loads:
        load.start()

    core_peer = (y_hi * 2 + 1 - core, s)
    other_f = (1 - y_hi) * 2 + core
    other_s = (x * 2 + 1 - y_lo) * 8 + z
    y_peers = [(other_f, s), (f, other_s), (other_f, other_s)]
    steps = sorted(
        [(dx, dz) for dx in range(4) for dz in range(8) if dx or dz],
        key=lambda t: -(min(t[0], 4 - t[0]) + min(t[1], 8 - t[1])),
    )
    places = [(lax.rem(x + dx, 4), lax.rem(z + dz, 8)) for dx, dz in steps]
    a2a_peers = [(f, (px * 2 + y_lo) * 8 + pz) for px, pz in places]

    barrier = pltpu.get_barrier_semaphore()
    everyone = a2a_peers + y_peers + [core_peer]
    for peer in everyone:
        pl.semaphore_signal(barrier, inc=1, device_id=peer, device_id_type=MESH)

    loads[0].wait()
    loads[1].wait()
    angle = phase[...]
    cosine = jnp.cos(angle)
    sine = jnp.sin(angle)
    weights = [
        [(group[k] == 2 * gh + gc).astype(F32) for gh in range(2) for gc in (1 - core, core)] for k in range(NFD)
    ]
    loads[2].wait()
    for a in range(8):
        lanes = slice(128 * a, 128 * a + 128)
        total = [[None, None] for _ in range(4)]
        for k in range(NFD):
            c = cosine[k : k + 1, lanes]
            d = sine[k : k + 1, lanes]
            re = refl[0, k, :, lanes]
            im = refl[1, k, :, lanes]
            turned = (re * c - im * d, re * d + im * c)
            for g in range(4):
                for part in range(2):
                    term = turned[part] * weights[k][g]
                    total[g][part] = term if k == 0 else total[g][part] + term
        for gh in range(2):
            for part in range(2):
                core_out[gh, part, :, lanes] = total[2 * gh][part]
                core_own[gh, part, :, lanes] = total[2 * gh + 1][part]

    pl.semaphore_wait(barrier, len(everyone))
    core_copy = pltpu.make_async_remote_copy(
        src_ref=core_out, dst_ref=core_in, send_sem=core_sem.at[0], recv_sem=core_sem.at[1],
        device_id=core_peer, device_id_type=MESH,
    )
    core_copy.start()
    loads[3].wait()
    loads[4].wait()
    core_copy.wait_recv()

    for gh in range(2):
        tiles = []
        for a in range(8):
            lanes = slice(128 * a, 128 * a + 128)
            tiles.append(tuple(core_own[gh, part, :, lanes] + core_in[gh, part, :, lanes] for part in range(2)))
        mixed = dft8(tiles)
        for k in range(8):
            vr, vi = mixed[k]
            c = twa[0, k : k + 1, :]
            d = twa[1, k : k + 1, :]
            first = gh * 128 + k * ROWS
            for part, value in enumerate((vr * c + vi * d, vi * c - vr * d)):
                hi, lo = halves(value)
                xsplit[0, first : first + ROWS, part * 128 : part * 128 + 128] = hi
                xsplit[1, first : first + ROWS, part * 128 : part * 128 + 128] = lo
    y = matmul_t(col[0], xsplit[0]) + (matmul_t(col[1], xsplit[0]) + matmul_t(col[0], xsplit[1]))
    for gh in range(2):
        for lo_index in range(2):
            y_out[gh, lo_index] = y[160 * lo_index : 160 * lo_index + 160, 128 * gh : 128 * gh + 128]

    y_copies = []
    for n, (gh, lo_index) in enumerate([(1 - y_hi, y_lo), (y_hi, 1 - y_lo), (1 - y_hi, 1 - y_lo)]):
        copy = pltpu.make_async_remote_copy(
            src_ref=y_out.at[gh, lo_index], dst_ref=y_in.at[n], send_sem=y_sem.at[0, n], recv_sem=y_sem.at[1, n],
            device_id=y_peers[n], device_id_type=MESH,
        )
        copy.start()
        y_copies.append(copy)
    for copy in y_copies:
        copy.wait_recv()
    low = lax.broadcasted_iota(jnp.int32, (8, 128), 0) < 4
    for t in range(20):
        rows = slice(8 * t, 8 * t + 8)
        near = y_out[y_hi, y_lo, rows, :] + y_in[0, rows, :]
        far = y_in[1, rows, :] + y_in[2, rows, :]
        b = 2 * t
        q_buf[b // 10, b % 10] = jnp.where(low, near, pltpu.roll(far, 4, 0))
        q_buf[b // 10, b % 10 + 1] = jnp.where(low, pltpu.roll(near, 4, 0), far)

    own = x * 8 + z
    for n, (px, pz) in enumerate(places):
        pltpu.make_async_remote_copy(
            src_ref=q_buf.at[px, pl.ds(pz, 3)], dst_ref=r_buf.at[:, own], send_sem=a2a_sem.at[0],
            recv_sem=a2a_sem.at[1], device_id=a2a_peers[n], device_id_type=MESH,
        ).start()
    for b in range(3):
        r_buf[b, own] = q_buf[x, z + b]
    for load in loads[5:]:
        load.wait()
    w_left = widths[0, 0]
    w_right = widths[0, 1]
    wait_bytes(r_buf.at[:, pl.ds(0, 31)], a2a_sem.at[1])

    for b in range(3):
        hi, lo = halves(r_buf[b].reshape(256, 128))
        rsplit[0, :, 128 * b : 128 * b + 128] = hi
        rsplit[1, :, 128 * b : 128 * b + 128] = lo
    mid = matmul(row[0], rsplit[0]) + (matmul(row[1], rsplit[0]) + matmul(row[0], rsplit[1]))
    for b in range(3):
        for q in range(2):
            vr = mid[64 * q : 64 * q + 64, 128 * b : 128 * b + 128]
            vi = mid[128 + 64 * q : 192 + 64 * q, 128 * b : 128 * b + 128]
            first = (b * 2 + q) * 64
            for part, value in enumerate((vr * twb[0] + vi * twb[1], vi * twb[0] - vr * twb[1])):
                hi, lo = halves(value)
                vsplit[0, first : first + 64, 128 * part : 128 * part + 128] = hi
                vsplit[1, first : first + 64, 128 * part : 128 * part + 128] = lo
    t_buf[...] = matmul(vsplit[0], last[0]) + (matmul(vsplit[1], last[0]) + matmul(vsplit[0], last[1]))

    k_lane = lax.rem(lax.broadcasted_iota(jnp.int32, (1, 128), 1), 8)
    keep = []
    for b in range(3):
        for q in range(2):
            column = k_lane + 8 * q
            if b == 0:
                keep.append((column >= 16 - w_left).astype(F32))
            elif b == 1:
                keep.append(jnp.ones((1, 128), F32))
            else:
                keep.append((column < w_right).astype(F32))

    def block(n):
        return (t_buf[64 * n : 64 * n + 64, 0:128], t_buf[64 * n : 64 * n + 64, 128:256])

    def group_sum(value, which):
        hi, lo = halves(value)
        return matmul(jnp.concatenate([hi, lo], axis=1), sums[which])

    def normalized(nr, ni):
        both = group_sum(jnp.concatenate([nr, ni], axis=0), 0)
        vr = both[0:64]
        vi = both[64:128]
        power = vr * vr + vi * vi
        mean = jnp.sum(jnp.sum(power, axis=0, keepdims=True), axis=1, keepdims=True) * (1.0 / (8 * N))
        scale = 1.0 / jnp.sqrt(power + mean + EPS)
        return (vr * scale, vi * scale)

    nr = jnp.zeros((64, 128), F32)
    ni = jnp.zeros((64, 128), F32)
    for n in range(6):
        tr, ti = block(n)
        nr = nr + tr * keep[n]
        ni = ni + ti * keep[n]
    ur, ui = normalized(nr, ni)
    for _ in range(ITERS):
        rows = []
        for n in range(6):
            tr, ti = block(n)
            rows.append(jnp.sum(ur * tr + ui * ti, axis=0, keepdims=True) * keep[n])
            rows.append(jnp.sum(ui * tr - ur * ti, axis=0, keepdims=True) * keep[n])
        rows.append(jnp.zeros((4, 128), F32))
        back = group_sum(jnp.concatenate(rows, axis=0), 1)
        nr = jnp.zeros((64, 128), F32)
        ni = jnp.zeros((64, 128), F32)
        for n in range(6):
            tr, ti = block(n)
            br = back[2 * n : 2 * n + 1, :]
            bi = back[2 * n + 1 : 2 * n + 2, :]
            nr = nr + (tr * br - ti * bi)
            ni = ni + (tr * bi + ti * br)
        ur, ui = normalized(nr, ni)

    fixed = [[], []]
    for q in range(2):
        tr, ti = block(2 + q)
        fixed[0].append(ur * tr + ui * ti)
        fixed[1].append(ur * ti - ui * tr)
    left = lax.broadcasted_iota(jnp.int32, (8, 128), 1) < 64
    for part in range(2):
        turned = jnp.concatenate(fixed[part], axis=0).T
        for p in range(8):
            first = turned[16 * p : 16 * p + 8]
            second = turned[16 * p + 8 : 16 * p + 16]
            out_ref[part, 0:8, 128 * p : 128 * p + 128] = jnp.where(left, first, pltpu.roll(second, 64, 1))
            out_ref[part, 8:16, 128 * p : 128 * p + 128] = jnp.where(left, pltpu.roll(first, 64, 1), second)

    core_copy.wait_send()
    for copy in y_copies:
        copy.wait_send()
    wait_bytes(r_buf.at[:, pl.ds(0, 31)], a2a_sem.at[0])


def local(reflection, phase, group_index, widths):
    consts = [jnp.asarray(t) for t in tables()]
    operands = [reflection, phase, group_index, widths] + consts
    in_specs = [pl.BlockSpec(memory_space=pl.ANY)] * len(operands)
    scratch = [
        pltpu.VMEM((2, NFD, ROWS, N), F32),
        pltpu.VMEM((NFD, N), F32),
        pltpu.SMEM((NFD,), jnp.int32),
        pltpu.SMEM((1, 2), jnp.int32),
        pltpu.VMEM((2, 8, 128), F32),
        pltpu.VMEM((2, 320, 256), BF16),
        pltpu.VMEM((2, 256, 256), BF16),
        pltpu.VMEM((2, 64, 128), F32),
        pltpu.VMEM((2, 256, 256), BF16),
        pltpu.VMEM((2, 256, 128), BF16),
        pltpu.VMEM((2, 2, ROWS, N), F32),
        pltpu.VMEM((2, 2, ROWS, N), F32),
        pltpu.VMEM((2, 2, ROWS, N), F32),
        pltpu.VMEM((2, 256, 256), BF16),
        pltpu.VMEM((2, 2, 160, 128), F32),
        pltpu.VMEM((3, 160, 128), F32),
        pltpu.VMEM((4, 10, 8, 128), F32),
        pltpu.VMEM((3, 32, 8, 128), F32),
        pltpu.VMEM((2, 256, 384), BF16),
        pltpu.VMEM((2, 384, 256), BF16),
        pltpu.VMEM((384, 256), F32),
        pltpu.SemaphoreType.DMA((10,)),
        pltpu.SemaphoreType.DMA((2,)),
        pltpu.SemaphoreType.DMA((2, 3)),
        pltpu.SemaphoreType.DMA((2,)),
    ]
    result = pl.pallas_call(
        kernel,
        out_shape=jax.ShapeDtypeStruct((2, ROWS, N), F32),
        in_specs=in_specs,
        out_specs=pl.BlockSpec(memory_space=pltpu.VMEM),
        scratch_shapes=scratch,
        name="focus",
        compiler_params=pltpu.CompilerParams(
            collective_id=0, has_side_effects=True, vmem_limit_bytes=56 * 1024 * 1024
        ),
    )(*operands)
    return jnp.swapaxes(result, 1, 2)[:, None]


def solution(mesh):
    in_specs = (P(None, "freq", "space", None), P("freq", None), P("freq"), P("space", None))
    out_specs = P(None, "freq", None, "space")
    return jax.shard_map(local, mesh=mesh, in_specs=in_specs, out_specs=out_specs, check_vma=False)
```

time: 84.7 us -> 34.8 us (0.41)
  the two profiles are of different devices: /device:TPU:0 before, /device:TPU:1 now
where the time goes in v1:
time: 34.8 us; the launch traced here: 34.7 us
  Pallas kernels  33.1 us (95%)
  local copies, waits for them, and re-layouts  1.57 us (5%)
    pallas_call x1, Pallas kernels, local(): pl.pallas_call(kernel, out_shape=jax.ShapeDtypeStruct((2, ROWS, N), F32),...  33.1 us
    unnamed x1, local copies, waits for them, and re-layouts  1.57 us

profile of v1, /device:TPU:1, one launch (start us, length us, event | category | flops | bytes accessed | tf_op | source)
XLA Modules:
  0.0 34.7 jit_solution(13175265671135498495)
XLA Ops:
  0.0 33.1 %focus.1 = f32[2,16,1024]{2,1,0:T(8,128)} custom-call(f32[2,8,16,1024]{3,2,1,0:T(8,128)} %refl_hbm.1, f32[8,1024]{1,0:T(8,128)} %phase_hbm.1, s32[8]{0:T(128)} %group_hbm.1, s32[1,2]{1,0:T(1,128)} %widths_hbm.1, f32[2,8,128]{2,1,0:T(8,128)} %constant.12.clone.twa_hbm, bf16[2,320,256]{2,1,0:T(8,128)(2,1)} %constant.13.clone.col_hbm, ...), custom_call_target="tpu_custom_call" | custom-call | tf_op jit(solution)/shard_map/focus/pallas_call | solution.py:375
  33.1 1.6 %copy.13 = f32[2,1,1024,16]{2,3,1,0:T(8,128)} copy(f32[2,1,1024,16]{2,3,1,0:T(8,128)} %bitcast.5) | data formatting | bytes 262144

commit v2 on v1

--- a/solution.py
+++ b/solution.py
@@ -120,11 +120,11 @@
 
 
 def kernel(
-    refl_hbm, phase_hbm, group_hbm, widths_hbm, twa_hbm, col_hbm, row_hbm, twb_hbm, last_hbm, sums_hbm,
-    out_ref,
-    refl, phase, group, widths, twa, col, row, twb, last, sums,
-    core_out, core_own, core_in, xsplit, y_out, y_in, q_buf, r_buf, rsplit, vsplit, t_buf,
-    load_sem, core_sem, y_sem, a2a_sem,
+    refl_hbm, phase_hbm, group_hbm, twa_hbm, col_hbm,
+    r_buf,
+    refl, phase, group, twa, col,
+    core_out, core_own, core_in, xsplit, y_out, y_in, q_buf,
+    load_sem, core_sem, y_sem, a2a_sem, plane_sem,
 ):
     f = lax.axis_index("freq")
     s = lax.axis_index("space")
@@ -139,7 +139,6 @@
         for n, (src, dst) in enumerate(
             [
                 (group_hbm, group), (phase_hbm, phase), (refl_hbm, refl), (twa_hbm, twa), (col_hbm, col),
-                (row_hbm.at[y_lo], row), (twb_hbm, twb), (last_hbm, last), (sums_hbm, sums), (widths_hbm, widths),
             ]
         )
     ]
@@ -150,16 +149,18 @@
     other_f = (1 - y_hi) * 2 + core
     other_s = (x * 2 + 1 - y_lo) * 8 + z
     y_peers = [(other_f, s), (f, other_s), (other_f, other_s)]
-    steps = sorted(
-        [(dx, dz) for dx in range(4) for dz in range(8) if dx or dz],
-        key=lambda t: -(min(t[0], 4 - t[0]) + min(t[1], 8 - t[1])),
+    dests = sorted(
+        [(px, pz) for px in range(4) for pz in range(8)], key=lambda t: (min(t[1], 4), (0, 1, 2, 2)[t[0]], t[1])
     )
-    places = [(lax.rem(x + dx, 4), lax.rem(z + dz, 8)) for dx, dz in steps]
-    a2a_peers = [(f, (px * 2 + y_lo) * 8 + pz) for px, pz in places]
+    a2a_peers = [(f, (px * 2 + y_lo) * 8 + pz) for px, pz in dests]
+    own = x * 8 + z
+    is_other = [own != px * 8 + pz for px, pz in dests]
 
     barrier = pltpu.get_barrier_semaphore()
-    everyone = a2a_peers + y_peers + [core_peer]
-    for peer in everyone:
+    z_ring = [(f, (x * 2 + y_lo) * 8 + lax.rem(z + d, 8)) for d in (4, 3, 5, 2, 6, 1, 7)]
+    x_ring = [(f, (lax.rem(x + d, 4) * 2 + y_lo) * 8 + z) for d in (2, 1, 3)]
+    first_peers = [core_peer] + y_peers + x_ring + z_ring
+    for peer in first_peers:
         pl.semaphore_signal(barrier, inc=1, device_id=peer, device_id_type=MESH)
 
     loads[0].wait()
@@ -189,12 +190,14 @@
                 core_out[gh, part, :, lanes] = total[2 * gh][part]
                 core_own[gh, part, :, lanes] = total[2 * gh + 1][part]
 
-    pl.semaphore_wait(barrier, len(everyone))
+    pl.semaphore_wait(barrier, len(first_peers))
     core_copy = pltpu.make_async_remote_copy(
         src_ref=core_out, dst_ref=core_in, send_sem=core_sem.at[0], recv_sem=core_sem.at[1],
         device_id=core_peer, device_id_type=MESH,
     )
     core_copy.start()
+    for peer in x_ring:
+        pl.semaphore_signal(plane_sem, inc=1, device_id=peer, device_id_type=MESH)
     loads[3].wait()
     loads[4].wait()
     core_copy.wait_recv()
@@ -227,6 +230,7 @@
         )
         copy.start()
         y_copies.append(copy)
+    pl.semaphore_wait(plane_sem, 3)
     for copy in y_copies:
         copy.wait_recv()
     low = lax.broadcasted_iota(jnp.int32, (8, 128), 0) < 4
@@ -238,20 +242,29 @@
         q_buf[b // 10, b % 10] = jnp.where(low, near, pltpu.roll(far, 4, 0))
         q_buf[b // 10, b % 10 + 1] = jnp.where(low, pltpu.roll(near, 4, 0), far)
 
-    own = x * 8 + z
-    for n, (px, pz) in enumerate(places):
-        pltpu.make_async_remote_copy(
-            src_ref=q_buf.at[px, pl.ds(pz, 3)], dst_ref=r_buf.at[:, own], send_sem=a2a_sem.at[0],
-            recv_sem=a2a_sem.at[1], device_id=a2a_peers[n], device_id_type=MESH,
-        ).start()
+    for other, peer, (px, pz) in zip(is_other, a2a_peers, dests):
+
+        @pl.when(other)
+        def _(peer=peer, px=px, pz=pz):
+            pltpu.make_async_remote_copy(
+                src_ref=q_buf.at[px, pl.ds(pz, 3)], dst_ref=r_buf.at[:, own], send_sem=a2a_sem.at[0],
+                recv_sem=a2a_sem.at[1], device_id=peer, device_id_type=MESH,
+            ).start()
+
     for b in range(3):
         r_buf[b, own] = q_buf[x, z + b]
-    for load in loads[5:]:
-        load.wait()
+    wait_bytes(r_buf.at[:, pl.ds(0, 31)], a2a_sem.at[1])
+
+    core_copy.wait_send()
+    for copy in y_copies:
+        copy.wait_send()
+    wait_bytes(r_buf.at[:, pl.ds(0, 31)], a2a_sem.at[0])
+
+
+def finish(r_buf, widths, row_all, twb, last, sums, out_ref, rsplit, vsplit, t_buf):
+    row = row_all.at[lax.rem(lax.axis_index("space") // 8, 2)]
     w_left = widths[0, 0]
     w_right = widths[0, 1]
-    wait_bytes(r_buf.at[:, pl.ds(0, 31)], a2a_sem.at[1])
-
     for b in range(3):
         hi, lo = halves(r_buf[b].reshape(256, 128))
         rsplit[0, :, 128 * b : 128 * b + 128] = hi
@@ -335,27 +348,17 @@
             out_ref[part, 0:8, 128 * p : 128 * p + 128] = jnp.where(left, first, pltpu.roll(second, 64, 1))
             out_ref[part, 8:16, 128 * p : 128 * p + 128] = jnp.where(left, pltpu.roll(first, 64, 1), second)
 
-    core_copy.wait_send()
-    for copy in y_copies:
-        copy.wait_send()
-    wait_bytes(r_buf.at[:, pl.ds(0, 31)], a2a_sem.at[0])
-
 
 def local(reflection, phase, group_index, widths):
-    consts = [jnp.asarray(t) for t in tables()]
-    operands = [reflection, phase, group_index, widths] + consts
-    in_specs = [pl.BlockSpec(memory_space=pl.ANY)] * len(operands)
+    twa, col, row, twb, last, sums = [jnp.asarray(t) for t in tables()]
+    anywhere = pl.BlockSpec(memory_space=pltpu.HBM)
+    vmem = pl.BlockSpec(memory_space=pltpu.VMEM)
     scratch = [
         pltpu.VMEM((2, NFD, ROWS, N), F32),
         pltpu.VMEM((NFD, N), F32),
         pltpu.SMEM((NFD,), jnp.int32),
-        pltpu.SMEM((1, 2), jnp.int32),
         pltpu.VMEM((2, 8, 128), F32),
         pltpu.VMEM((2, 320, 256), BF16),
-        pltpu.VMEM((2, 256, 256), BF16),
-        pltpu.VMEM((2, 64, 128), F32),
-        pltpu.VMEM((2, 256, 256), BF16),
-        pltpu.VMEM((2, 256, 128), BF16),
         pltpu.VMEM((2, 2, ROWS, N), F32),
         pltpu.VMEM((2, 2, ROWS, N), F32),
         pltpu.VMEM((2, 2, ROWS, N), F32),
@@ -363,26 +366,37 @@
         pltpu.VMEM((2, 2, 160, 128), F32),
         pltpu.VMEM((3, 160, 128), F32),
         pltpu.VMEM((4, 10, 8, 128), F32),
-        pltpu.VMEM((3, 32, 8, 128), F32),
-        pltpu.VMEM((2, 256, 384), BF16),
-        pltpu.VMEM((2, 384, 256), BF16),
-        pltpu.VMEM((384, 256), F32),
         pltpu.SemaphoreType.DMA((10,)),
         pltpu.SemaphoreType.DMA((2,)),
         pltpu.SemaphoreType.DMA((2, 3)),
         pltpu.SemaphoreType.DMA((2,)),
+        pltpu.SemaphoreType.REGULAR,
     ]
-    result = pl.pallas_call(
+    gathered = pl.pallas_call(
         kernel,
-        out_shape=jax.ShapeDtypeStruct((2, ROWS, N), F32),
-        in_specs=in_specs,
-        out_specs=pl.BlockSpec(memory_space=pltpu.VMEM),
+        out_shape=jax.ShapeDtypeStruct((3, 32, 8, 128), F32),
+        in_specs=[anywhere] * 5,
+        out_specs=vmem,
         scratch_shapes=scratch,
         name="focus",
         compiler_params=pltpu.CompilerParams(
-            collective_id=0, has_side_effects=True, vmem_limit_bytes=56 * 1024 * 1024
+            collective_id=0, has_side_effects=True, vmem_limit_bytes=48 * 1024 * 1024
         ),
-    )(*operands)
+    )(*[pltpu.with_memory_space_constraint(v, pltpu.HBM) for v in (reflection, phase, group_index, twa, col)])
+
+    result = pl.pallas_call(
+        finish,
+        out_shape=jax.ShapeDtypeStruct((2, ROWS, N), F32),
+        in_specs=[vmem, pl.BlockSpec(memory_space=pltpu.SMEM), vmem, vmem, vmem, vmem],
+        out_specs=vmem,
+        scratch_shapes=[
+            pltpu.VMEM((2, 256, 384), BF16),
+            pltpu.VMEM((2, 384, 256), BF16),
+            pltpu.VMEM((384, 256), F32),
+        ],
+        name="finish",
+        compiler_params=pltpu.CompilerParams(vmem_limit_bytes=48 * 1024 * 1024),
+    )(gathered, widths, row, twb, last, sums)
     return jnp.swapaxes(result, 1, 2)[:, None]
 
 

time: 34.8 us -> 31.7 us (0.911)
  the two profiles are of different devices: /device:TPU:1 before, /device:TPU:64 now
where the time goes in v2:
time: 31.7 us; the launch traced here: 31.6 us
  Pallas kernels  31.5 us (99%)
    pallas_call x1, Pallas kernels, local(): pl.pallas_call(kernel, out_shape=jax.ShapeDtypeStruct((3, 32, 8, 128), F3...  27.6 us
    pallas_call x1, Pallas kernels, local(): pl.pallas_call(finish, out_shape=jax.ShapeDtypeStruct((2, ROWS, N), F32),...  3.92 us

profile of v2, /device:TPU:64, one launch (start us, length us, event | category | flops | bytes accessed | tf_op | source)
XLA Modules:
  0.0 31.6 jit_solution(11928690648872568521)
XLA Ops:
  0.0 0.0 copy-start
  0.0 0.0 copy-start.1
  0.0 0.0 copy-start.2
  0.0 0.0 copy-start.3
  0.0 0.0 copy-start.4
  0.0 27.6 %focus.1.r_buf = f32[3,32,8,128]{3,2,1,0:T(8,128)S(1)} custom-call(f32[2,8,16,1024]{3,2,1,0:T(8,128)} %refl_hbm.1, f32[8,1024]{1,0:T(8,128)} %phase_hbm.1, s32[8]{0:T(128)} %group_hbm.1, f32[2,8,128]{2,1,0:T(8,128)} %constant.12.clone.twa_hbm, bf16[2,320,256]{2,1,0:T(8,128)(2,1)} %constant.13.clone.col_hbm), custom_call_target="tpu_custom_call" | custom-call | tf_op jit(solution)/shard_map/focus/pallas_call | solution.py:375
  27.6 0.0 copy-done
  27.6 0.0 copy-done.1
  27.6 0.0 copy-done.2
  27.6 0.0 copy-done.3
  27.6 0.0 copy-done.4
  27.7 3.9 %finish.1 = f32[2,16,1024]{2,1,0:T(8,128)} custom-call(f32[3,32,8,128]{3,2,1,0:T(8,128)S(1)} %focus.1.r_buf, s32[1,2]{1,0:T(1,128)S(1)} %copy-done.4, bf16[2,2,256,256]{3,2,1,0:T(8,128)(2,1)S(1)} %copy-done, f32[2,64,128]{2,1,0:T(8,128)S(1)} %copy-done.3, bf16[2,256,256]{2,1,0:T(8,128)(2,1)S(1)} %copy-done.1, bf16[2,256,128]{2,1,0:T(8,128)(2,1)S(1)} %copy-done.2), custom_call_target="tpu_custom_call" | custom-call | tf_op jit(solution)/shard_map/finish/pallas_call | solution.py:387
Async XLA Ops:
  0.0 27.6 %copy-start = (bf16[2,2,256,256]{3,2,1,0:T(8,128)(2,1)S(1)}, bf16[2,2,256,256]{3,2,1,0:T(8,128)(2,1)}, u32[]{:S(2)}) copy-start(bf16[2,2,256,256]{3,2,1,0:T(8,128)(2,1)} %constant.14.clone.row_all) | copy-start | bytes 1572868
  0.0 27.6 %copy-start.1 = (bf16[2,256,256]{2,1,0:T(8,128)(2,1)S(1)}, bf16[2,256,256]{2,1,0:T(8,128)(2,1)}, u32[]{:S(2)}) copy-start(bf16[2,256,256]{2,1,0:T(8,128)(2,1)} %constant.16.clone.last) | copy-start | bytes 786436
  0.0 27.6 %copy-start.2 = (bf16[2,256,128]{2,1,0:T(8,128)(2,1)S(1)}, bf16[2,256,128]{2,1,0:T(8,128)(2,1)}, u32[]{:S(2)}) copy-start(bf16[2,256,128]{2,1,0:T(8,128)(2,1)} %constant.17.clone.sums) | copy-start | bytes 393220
  0.0 27.6 %copy-start.3 = (f32[2,64,128]{2,1,0:T(8,128)S(1)}, f32[2,64,128]{2,1,0:T(8,128)}, u32[]{:S(2)}) copy-start(f32[2,64,128]{2,1,0:T(8,128)} %constant.15.clone.twb) | copy-start | bytes 196612
  0.0 27.6 %copy-start.4 = (s32[1,2]{1,0:T(1,128)S(1)}, s32[1,2]{1,0:T(1,128)}, u32[]{:S(2)}) copy-start(s32[1,2]{1,0:T(1,128)} %widths.1) | copy-start | bytes 28

commit v3 on v1

--- a/solution.py
+++ b/solution.py
@@ -31,8 +31,8 @@
     k1 = np.arange(8)
     ang = 2 * np.pi * (k1[:, None] * lane[None, :] % N) / N
     twist_a = np.stack([np.cos(ang), np.sin(ang)]) / 32.0
-    y_lo, x, slot, q_hi = np.meshgrid(np.arange(2), np.arange(4), np.arange(10), np.arange(2), indexing="ij")
-    block = ((x * 2 + y_lo) * 8 + slot - 1) % 64
+    half, y_lo, x, slot, q_hi = np.meshgrid(*[np.arange(n) for n in (2, 2, 4, 5, 2)], indexing="ij")
+    block = ((x * 2 + y_lo) * 8 + half * 5 + slot - 1) % 64
     k2 = (2 * block + q_hi).reshape(-1)
     ang = 2 * np.pi * (k2[:, None] * lane[None, :] % 128) / 128
     cos, sin = (np.cos(ang), np.sin(ang))
@@ -124,7 +124,7 @@
     out_ref,
     refl, phase, group, widths, twa, col, row, twb, last, sums,
     core_out, core_own, core_in, xsplit, y_out, y_in, q_buf, r_buf, rsplit, vsplit, t_buf,
-    load_sem, core_sem, y_sem, a2a_sem,
+    load_sem, core_sem, y_sem, a2a_sem, plane_sem,
 ):
     f = lax.axis_index("freq")
     s = lax.axis_index("space")
@@ -150,16 +150,14 @@
     other_f = (1 - y_hi) * 2 + core
     other_s = (x * 2 + 1 - y_lo) * 8 + z
     y_peers = [(other_f, s), (f, other_s), (other_f, other_s)]
-    steps = sorted(
-        [(dx, dz) for dx in range(4) for dz in range(8) if dx or dz],
-        key=lambda t: -(min(t[0], 4 - t[0]) + min(t[1], 8 - t[1])),
-    )
-    places = [(lax.rem(x + dx, 4), lax.rem(z + dz, 8)) for dx, dz in steps]
-    a2a_peers = [(f, (px * 2 + y_lo) * 8 + pz) for px, pz in places]
+    own = x * 8 + z
+    dests = [(dx, pz) for pz in (0, 1, 2, 3, 4, 5, 6, 7) for dx in (2, 1, 3, 0)]
 
     barrier = pltpu.get_barrier_semaphore()
-    everyone = a2a_peers + y_peers + [core_peer]
-    for peer in everyone:
+    z_ring = [(f, (x * 2 + y_lo) * 8 + lax.rem(z + d, 8)) for d in (4, 3, 5, 2, 6, 1, 7)]
+    x_ring = [(f, (lax.rem(x + d, 4) * 2 + y_lo) * 8 + z) for d in (2, 1, 3)]
+    first_peers = [core_peer] + y_peers + x_ring + z_ring
+    for peer in first_peers:
         pl.semaphore_signal(barrier, inc=1, device_id=peer, device_id_type=MESH)
 
     loads[0].wait()
@@ -189,17 +187,42 @@
                 core_out[gh, part, :, lanes] = total[2 * gh][part]
                 core_own[gh, part, :, lanes] = total[2 * gh + 1][part]
 
-    pl.semaphore_wait(barrier, len(everyone))
-    core_copy = pltpu.make_async_remote_copy(
-        src_ref=core_out, dst_ref=core_in, send_sem=core_sem.at[0], recv_sem=core_sem.at[1],
-        device_id=core_peer, device_id_type=MESH,
-    )
-    core_copy.start()
+    pl.semaphore_wait(barrier, len(first_peers))
+    groups = (1 - y_hi, y_hi)
+    core_copies = [
+        pltpu.make_async_remote_copy(
+            src_ref=core_out.at[gh], dst_ref=core_in.at[gh], send_sem=core_sem.at[0, n], recv_sem=core_sem.at[1, n],
+            device_id=core_peer, device_id_type=MESH,
+        )
+        for n, gh in enumerate(groups)
+    ]
+    for copy in core_copies:
+        copy.start()
+    for peer in x_ring:
+        pl.semaphore_signal(plane_sem, inc=1, device_id=peer, device_id_type=MESH)
     loads[3].wait()
     loads[4].wait()
-    core_copy.wait_recv()
-
-    for gh in range(2):
+
+    y_copies = []
+
+    def y_part(half, n):
+        rows = slice(160 * half, 160 * half + 160)
+        y = matmul_t(col[0, rows], xsplit[n, 0]) + (
+            matmul_t(col[1, rows], xsplit[n, 0]) + matmul_t(col[0, rows], xsplit[n, 1])
+        )
+        for index in range(2):
+            y_out[half, n, index] = y[80 * index : 80 * index + 80]
+        for place, peer in ((y_lo, y_peers[0]), (1 - y_lo, y_peers[2])) if n == 0 else ((1 - y_lo, y_peers[1]),):
+            slot = len(y_copies)
+            copy = pltpu.make_async_remote_copy(
+                src_ref=y_out.at[half, n, place], dst_ref=y_in.at[slot], send_sem=y_sem.at[0, slot],
+                recv_sem=y_sem.at[1, slot], device_id=peer, device_id_type=MESH,
+            )
+            copy.start()
+            y_copies.append(copy)
+
+    for n, gh in enumerate(groups):
+        core_copies[n].wait_recv()
         tiles = []
         for a in range(8):
             lanes = slice(128 * a, 128 * a + 128)
@@ -209,41 +232,42 @@
             vr, vi = mixed[k]
             c = twa[0, k : k + 1, :]
             d = twa[1, k : k + 1, :]
-            first = gh * 128 + k * ROWS
+            first = k * ROWS
             for part, value in enumerate((vr * c + vi * d, vi * c - vr * d)):
                 hi, lo = halves(value)
-                xsplit[0, first : first + ROWS, part * 128 : part * 128 + 128] = hi
-                xsplit[1, first : first + ROWS, part * 128 : part * 128 + 128] = lo
-    y = matmul_t(col[0], xsplit[0]) + (matmul_t(col[1], xsplit[0]) + matmul_t(col[0], xsplit[1]))
-    for gh in range(2):
-        for lo_index in range(2):
-            y_out[gh, lo_index] = y[160 * lo_index : 160 * lo_index + 160, 128 * gh : 128 * gh + 128]
-
-    y_copies = []
-    for n, (gh, lo_index) in enumerate([(1 - y_hi, y_lo), (y_hi, 1 - y_lo), (1 - y_hi, 1 - y_lo)]):
-        copy = pltpu.make_async_remote_copy(
-            src_ref=y_out.at[gh, lo_index], dst_ref=y_in.at[n], send_sem=y_sem.at[0, n], recv_sem=y_sem.at[1, n],
-            device_id=y_peers[n], device_id_type=MESH,
-        )
-        copy.start()
-        y_copies.append(copy)
-    for copy in y_copies:
-        copy.wait_recv()
+                xsplit[n, 0, first : first + ROWS, part * 128 : part * 128 + 128] = hi
+                xsplit[n, 1, first : first + ROWS, part * 128 : part * 128 + 128] = lo
+        y_part(0, n)
+    for n in range(2):
+        y_part(1, n)
+    pl.semaphore_wait(plane_sem, 3)
+
     low = lax.broadcasted_iota(jnp.int32, (8, 128), 0) < 4
-    for t in range(20):
-        rows = slice(8 * t, 8 * t + 8)
-        near = y_out[y_hi, y_lo, rows, :] + y_in[0, rows, :]
-        far = y_in[1, rows, :] + y_in[2, rows, :]
-        b = 2 * t
-        q_buf[b // 10, b % 10] = jnp.where(low, near, pltpu.roll(far, 4, 0))
-        q_buf[b // 10, b % 10 + 1] = jnp.where(low, pltpu.roll(near, 4, 0), far)
-
-    own = x * 8 + z
-    for n, (px, pz) in enumerate(places):
-        pltpu.make_async_remote_copy(
-            src_ref=q_buf.at[px, pl.ds(pz, 3)], dst_ref=r_buf.at[:, own], send_sem=a2a_sem.at[0],
-            recv_sem=a2a_sem.at[1], device_id=a2a_peers[n], device_id_type=MESH,
-        ).start()
+    for half in range(2):
+        for copy in y_copies[3 * half : 3 * half + 3]:
+            copy.wait_recv()
+        for t in range(10):
+            rows = slice(8 * t, 8 * t + 8)
+            near = y_out[half, 1, y_lo, rows, :] + y_in[3 * half, rows, :]
+            far = y_in[3 * half + 1, rows, :] + y_in[3 * half + 2, rows, :]
+            n = 2 * t
+            q_buf[n // 5, half * 5 + n % 5] = jnp.where(low, near, pltpu.roll(far, 4, 0))
+            n = n + 1
+            q_buf[n // 5, half * 5 + n % 5] = jnp.where(low, pltpu.roll(near, 4, 0), far)
+
+        for dx, pz in [d for d in dests if (d[1] >= 3) == (half == 1)]:
+            px = lax.rem(x + dx, 4)
+
+            def push(px=px, pz=pz):
+                pltpu.make_async_remote_copy(
+                    src_ref=q_buf.at[px, pl.ds(pz, 3)], dst_ref=r_buf.at[:, own], send_sem=a2a_sem.at[0],
+                    recv_sem=a2a_sem.at[1], device_id=(f, (px * 2 + y_lo) * 8 + pz), device_id_type=MESH,
+                ).start()
+
+            if dx:
+                push()
+            else:
+                pl.when(z != pz)(push)
     for b in range(3):
         r_buf[b, own] = q_buf[x, z + b]
     for load in loads[5:]:
@@ -335,8 +359,7 @@
             out_ref[part, 0:8, 128 * p : 128 * p + 128] = jnp.where(left, first, pltpu.roll(second, 64, 1))
             out_ref[part, 8:16, 128 * p : 128 * p + 128] = jnp.where(left, pltpu.roll(first, 64, 1), second)
 
-    core_copy.wait_send()
-    for copy in y_copies:
+    for copy in core_copies + y_copies:
         copy.wait_send()
     wait_bytes(r_buf.at[:, pl.ds(0, 31)], a2a_sem.at[0])
 
@@ -344,7 +367,8 @@
 def local(reflection, phase, group_index, widths):
     consts = [jnp.asarray(t) for t in tables()]
     operands = [reflection, phase, group_index, widths] + consts
-    in_specs = [pl.BlockSpec(memory_space=pl.ANY)] * len(operands)
+    operands = [pltpu.with_memory_space_constraint(v, pltpu.HBM) for v in operands]
+    in_specs = [pl.BlockSpec(memory_space=pltpu.HBM)] * len(operands)
     scratch = [
         pltpu.VMEM((2, NFD, ROWS, N), F32),
         pltpu.VMEM((NFD, N), F32),
@@ -359,18 +383,19 @@
         pltpu.VMEM((2, 2, ROWS, N), F32),
         pltpu.VMEM((2, 2, ROWS, N), F32),
         pltpu.VMEM((2, 2, ROWS, N), F32),
-        pltpu.VMEM((2, 256, 256), BF16),
-        pltpu.VMEM((2, 2, 160, 128), F32),
-        pltpu.VMEM((3, 160, 128), F32),
+        pltpu.VMEM((2, 2, 128, 256), BF16),
+        pltpu.VMEM((2, 2, 2, 80, 128), F32),
+        pltpu.VMEM((6, 80, 128), F32),
         pltpu.VMEM((4, 10, 8, 128), F32),
         pltpu.VMEM((3, 32, 8, 128), F32),
         pltpu.VMEM((2, 256, 384), BF16),
         pltpu.VMEM((2, 384, 256), BF16),
         pltpu.VMEM((384, 256), F32),
         pltpu.SemaphoreType.DMA((10,)),
+        pltpu.SemaphoreType.DMA((2, 2)),
+        pltpu.SemaphoreType.DMA((2, 6)),
         pltpu.SemaphoreType.DMA((2,)),
-        pltpu.SemaphoreType.DMA((2, 3)),
-        pltpu.SemaphoreType.DMA((2,)),
+        pltpu.SemaphoreType.REGULAR,
     ]
     result = pl.pallas_call(
         kernel,
@@ -380,7 +405,7 @@
         scratch_shapes=scratch,
         name="focus",
         compiler_params=pltpu.CompilerParams(
-            collective_id=0, has_side_effects=True, vmem_limit_bytes=56 * 1024 * 1024
+            collective_id=0, has_side_effects=True, vmem_limit_bytes=48 * 1024 * 1024
         ),
     )(*operands)
     return jnp.swapaxes(result, 1, 2)[:, None]

time: 34.8 us -> 29.6 us (0.85)
  the two profiles are of different devices: /device:TPU:1 before, /device:TPU:192 now
where the time goes in v3:
time: 29.6 us; the launch traced here: 29.5 us
  Pallas kernels  28.9 us (98%)
  local copies, waits for them, and re-layouts  0.66 us (2%)
    pallas_call x1, Pallas kernels, local(): pl.pallas_call(kernel, out_shape=jax.ShapeDtypeStruct((2, ROWS, N), F32),...  28.9 us
    unnamed x1, local copies, waits for them, and re-layouts  0.66 us

profile of v3, /device:TPU:192, one launch (start us, length us, event | category | flops | bytes accessed | tf_op | source)
XLA Modules:
  0.0 29.5 jit_solution(10358824558493591676)
XLA Ops:
  0.0 28.9 %focus.1 = f32[2,16,1024]{2,1,0:T(8,128)S(1)} custom-call(f32[2,8,16,1024]{3,2,1,0:T(8,128)} %refl_hbm.1, f32[8,1024]{1,0:T(8,128)} %phase_hbm.1, s32[8]{0:T(128)} %group_hbm.1, s32[1,2]{1,0:T(1,128)} %widths_hbm.1, f32[2,8,128]{2,1,0:T(8,128)} %constant.12.clone.twa_hbm, bf16[2,320,256]{2,1,0:T(8,128)(2,1)} %constant.13.clone.col_hbm, ...), custom_call_target="tpu_custom_call" | custom-call | tf_op jit(solution)/shard_map/focus/pallas_call | solution.py:400
  28.9 0.7 %copy.13 = f32[2,1,1024,16]{2,3,1,0:T(8,128)} copy(f32[2,1,1024,16]{2,3,1,0:T(8,128)S(1)} %bitcast.5) | data formatting | bytes 262144

commit v4 on v3

--- a/solution.py
+++ b/solution.py
@@ -18,6 +18,7 @@
 NFD = 8
 ROWS = 16
 EPS = 1e-06
+CHUNKS = ((0, 3), (3, 2), (5, 2), (7, 3))
 
 
 def split_np(table):
@@ -31,9 +32,11 @@
     k1 = np.arange(8)
     ang = 2 * np.pi * (k1[:, None] * lane[None, :] % N) / N
     twist_a = np.stack([np.cos(ang), np.sin(ang)]) / 32.0
-    half, y_lo, x, slot, q_hi = np.meshgrid(*[np.arange(n) for n in (2, 2, 4, 5, 2)], indexing="ij")
-    block = ((x * 2 + y_lo) * 8 + half * 5 + slot - 1) % 64
-    k2 = (2 * block + q_hi).reshape(-1)
+    k2 = []
+    for first, count in CHUNKS:
+        y_lo, x, slot, q_hi = np.meshgrid(np.arange(2), np.arange(4), first + np.arange(count), np.arange(2), indexing="ij")
+        k2.append((2 * (((x * 2 + y_lo) * 8 + slot - 1) % 64) + q_hi).reshape(-1))
+    k2 = np.concatenate(k2)
     ang = 2 * np.pi * (k2[:, None] * lane[None, :] % 128) / 128
     cos, sin = (np.cos(ang), np.sin(ang))
     real_rows = np.concatenate([cos, sin], axis=1)
@@ -206,16 +209,18 @@
     y_copies = []
 
     def y_part(half, n):
-        rows = slice(160 * half, 160 * half + 160)
+        first, count = CHUNKS[half]
+        rows = slice(32 * first, 32 * (first + count))
         y = matmul_t(col[0, rows], xsplit[n, 0]) + (
             matmul_t(col[1, rows], xsplit[n, 0]) + matmul_t(col[0, rows], xsplit[n, 1])
         )
         for index in range(2):
-            y_out[half, n, index] = y[80 * index : 80 * index + 80]
+            y_out[n, index, 16 * first : 16 * (first + count)] = y[16 * count * index : 16 * count * (index + 1)]
         for place, peer in ((y_lo, y_peers[0]), (1 - y_lo, y_peers[2])) if n == 0 else ((1 - y_lo, y_peers[1]),):
             slot = len(y_copies)
+            part = pl.ds(16 * first, 16 * count)
             copy = pltpu.make_async_remote_copy(
-                src_ref=y_out.at[half, n, place], dst_ref=y_in.at[slot], send_sem=y_sem.at[0, slot],
+                src_ref=y_out.at[n, place, part], dst_ref=y_in.at[slot % 3, part], send_sem=y_sem.at[0, slot],
                 recv_sem=y_sem.at[1, slot], device_id=peer, device_id_type=MESH,
             )
             copy.start()
@@ -238,24 +243,25 @@
                 xsplit[n, 0, first : first + ROWS, part * 128 : part * 128 + 128] = hi
                 xsplit[n, 1, first : first + ROWS, part * 128 : part * 128 + 128] = lo
         y_part(0, n)
-    for n in range(2):
-        y_part(1, n)
+    for half in range(1, len(CHUNKS)):
+        for n in range(2):
+            y_part(half, n)
     pl.semaphore_wait(plane_sem, 3)
 
     low = lax.broadcasted_iota(jnp.int32, (8, 128), 0) < 4
-    for half in range(2):
+    for half, (first, count) in enumerate(CHUNKS):
         for copy in y_copies[3 * half : 3 * half + 3]:
             copy.wait_recv()
-        for t in range(10):
-            rows = slice(8 * t, 8 * t + 8)
-            near = y_out[half, 1, y_lo, rows, :] + y_in[3 * half, rows, :]
-            far = y_in[3 * half + 1, rows, :] + y_in[3 * half + 2, rows, :]
+        for t in range(2 * count):
+            rows = slice(16 * first + 8 * t, 16 * first + 8 * t + 8)
+            near = y_out[1, y_lo, rows, :] + y_in[0, rows, :]
+            far = y_in[1, rows, :] + y_in[2, rows, :]
             n = 2 * t
-            q_buf[n // 5, half * 5 + n % 5] = jnp.where(low, near, pltpu.roll(far, 4, 0))
+            q_buf[n // count, first + n % count] = jnp.where(low, near, pltpu.roll(far, 4, 0))
             n = n + 1
-            q_buf[n // 5, half * 5 + n % 5] = jnp.where(low, pltpu.roll(near, 4, 0), far)
-
-        for dx, pz in [d for d in dests if (d[1] >= 3) == (half == 1)]:
+            q_buf[n // count, first + n % count] = jnp.where(low, pltpu.roll(near, 4, 0), far)
+
+        for dx, pz in [d for d in dests if first <= d[1] + 2 < first + count]:
             px = lax.rem(x + dx, 4)
 
             def push(px=px, pz=pz):
@@ -384,8 +390,8 @@
         pltpu.VMEM((2, 2, ROWS, N), F32),
         pltpu.VMEM((2, 2, ROWS, N), F32),
         pltpu.VMEM((2, 2, 128, 256), BF16),
-        pltpu.VMEM((2, 2, 2, 80, 128), F32),
-        pltpu.VMEM((6, 80, 128), F32),
+        pltpu.VMEM((2, 2, 160, 128), F32),
+        pltpu.VMEM((3, 160, 128), F32),
         pltpu.VMEM((4, 10, 8, 128), F32),
         pltpu.VMEM((3, 32, 8, 128), F32),
         pltpu.VMEM((2, 256, 384), BF16),
@@ -393,7 +399,7 @@
         pltpu.VMEM((384, 256), F32),
         pltpu.SemaphoreType.DMA((10,)),
         pltpu.SemaphoreType.DMA((2, 2)),
-        pltpu.SemaphoreType.DMA((2, 6)),
+        pltpu.SemaphoreType.DMA((2, 3 * len(CHUNKS))),
         pltpu.SemaphoreType.DMA((2,)),
         pltpu.SemaphoreType.REGULAR,
     ]

time: 29.6 us -> 28.5 us (0.963)
  the two profiles are of different devices: /device:TPU:192 before, /device:TPU:224 now
where the time goes in v4:
time: 28.5 us; the launch traced here: 28.4 us
  Pallas kernels  27.7 us (97%)
  local copies, waits for them, and re-layouts  0.66 us (2%)
    pallas_call x1, Pallas kernels, local(): pl.pallas_call(kernel, out_shape=jax.ShapeDtypeStruct((2, ROWS, N), F32),...  27.7 us
    unnamed x1, local copies, waits for them, and re-layouts  0.66 us

profile of v4, /device:TPU:224, one launch (start us, length us, event | category | flops | bytes accessed | tf_op | source)
XLA Modules:
  0.0 28.4 jit_solution(10485987808826463803)
XLA Ops:
  0.0 27.7 %focus.1 = f32[2,16,1024]{2,1,0:T(8,128)S(1)} custom-call(f32[2,8,16,1024]{3,2,1,0:T(8,128)} %refl_hbm.1, f32[8,1024]{1,0:T(8,128)} %phase_hbm.1, s32[8]{0:T(128)} %group_hbm.1, s32[1,2]{1,0:T(1,128)} %widths_hbm.1, f32[2,8,128]{2,1,0:T(8,128)} %constant.12.clone.twa_hbm, bf16[2,320,256]{2,1,0:T(8,128)(2,1)} %constant.13.clone.col_hbm, ...), custom_call_target="tpu_custom_call" | custom-call | tf_op jit(solution)/shard_map/focus/pallas_call | solution.py:406
  27.7 0.7 %copy.13 = f32[2,1,1024,16]{2,3,1,0:T(8,128)} copy(f32[2,1,1024,16]{2,3,1,0:T(8,128)S(1)} %bitcast.5) | data formatting | bytes 262144

commit v5 on v4

--- a/solution.py
+++ b/solution.py
@@ -137,6 +137,19 @@
     y_lo = lax.rem(s // 8, 2)
     z = lax.rem(s, 8)
 
+    core_peer = (y_hi * 2 + 1 - core, s)
+    other_f = (1 - y_hi) * 2 + core
+    other_s = (x * 2 + 1 - y_lo) * 8 + z
+    y_peers = [(other_f, s), (f, other_s), (other_f, other_s)]
+    own = x * 8 + z
+
+    barrier = pltpu.get_barrier_semaphore()
+    z_ring = [(f, (x * 2 + y_lo) * 8 + lax.rem(z + d, 8)) for d in (4, 3, 5, 2, 6, 1, 7)]
+    x_ring = [(f, (lax.rem(x + d, 4) * 2 + y_lo) * 8 + z) for d in (2, 1, 3)]
+    first_peers = z_ring[:3] + y_peers[:1] + x_ring[:1] + z_ring[3:] + y_peers[1:] + x_ring[1:] + [core_peer]
+    for peer in first_peers:
+        pl.semaphore_signal(barrier, inc=1, device_id=peer, device_id_type=MESH)
+
     loads = [
         pltpu.make_async_copy(src, dst, load_sem.at[n])
         for n, (src, dst) in enumerate(
@@ -148,20 +161,6 @@
     ]
     for load in loads:
         load.start()
-
-    core_peer = (y_hi * 2 + 1 - core, s)
-    other_f = (1 - y_hi) * 2 + core
-    other_s = (x * 2 + 1 - y_lo) * 8 + z
-    y_peers = [(other_f, s), (f, other_s), (other_f, other_s)]
-    own = x * 8 + z
-    dests = [(dx, pz) for pz in (0, 1, 2, 3, 4, 5, 6, 7) for dx in (2, 1, 3, 0)]
-
-    barrier = pltpu.get_barrier_semaphore()
-    z_ring = [(f, (x * 2 + y_lo) * 8 + lax.rem(z + d, 8)) for d in (4, 3, 5, 2, 6, 1, 7)]
-    x_ring = [(f, (lax.rem(x + d, 4) * 2 + y_lo) * 8 + z) for d in (2, 1, 3)]
-    first_peers = [core_peer] + y_peers + x_ring + z_ring
-    for peer in first_peers:
-        pl.semaphore_signal(barrier, inc=1, device_id=peer, device_id_type=MESH)
 
     loads[0].wait()
     loads[1].wait()
@@ -261,8 +260,9 @@
             n = n + 1
             q_buf[n // count, first + n % count] = jnp.where(low, pltpu.roll(near, 4, 0), far)
 
-        for dx, pz in [d for d in dests if first <= d[1] + 2 < first + count]:
-            px = lax.rem(x + dx, 4)
+        now = [pz for pz in range(8) if first <= pz + 2 < first + count]
+        for dx, pz in [(None, pz) for pz in now] + [(dx, pz) for pz in now for dx in (2, 1, 3, 0)]:
+            px = 0 if dx is None else lax.rem(x + dx, 4)
 
             def push(px=px, pz=pz):
                 pltpu.make_async_remote_copy(
@@ -270,10 +270,8 @@
                     recv_sem=a2a_sem.at[1], device_id=(f, (px * 2 + y_lo) * 8 + pz), device_id_type=MESH,
                 ).start()
 
-            if dx:
-                push()
-            else:
-                pl.when(z != pz)(push)
+            other = own != px * 8 + pz
+            pl.when(other if dx is None else jnp.logical_and(px != 0, other))(push)
     for b in range(3):
         r_buf[b, own] = q_buf[x, z + b]
     for load in loads[5:]:

time: 28.5 us -> 27.8 us (0.975)
  the two profiles are of different devices: /device:TPU:224 before, /device:TPU:226 now
where the time goes in v5:
time: 27.8 us; the launch traced here: 27.6 us
  Pallas kernels  27 us (97%)
  local copies, waits for them, and re-layouts  0.66 us (2%)
    pallas_call x1, Pallas kernels, local(): pl.pallas_call(kernel, out_shape=jax.ShapeDtypeStruct((2, ROWS, N), F32),...  27 us
    unnamed x1, local copies, waits for them, and re-layouts  0.66 us

profile of v5, /device:TPU:226, one launch (start us, length us, event | category | flops | bytes accessed | tf_op | source)
XLA Modules:
  0.0 27.6 jit_solution(7203309669233312858)
XLA Ops:
  0.0 27.0 %focus.1 = f32[2,16,1024]{2,1,0:T(8,128)S(1)} custom-call(f32[2,8,16,1024]{3,2,1,0:T(8,128)} %refl_hbm.1, f32[8,1024]{1,0:T(8,128)} %phase_hbm.1, s32[8]{0:T(128)} %group_hbm.1, s32[1,2]{1,0:T(1,128)} %widths_hbm.1, f32[2,8,128]{2,1,0:T(8,128)} %constant.12.clone.twa_hbm, bf16[2,320,256]{2,1,0:T(8,128)(2,1)} %constant.13.clone.col_hbm, ...), custom_call_target="tpu_custom_call" | custom-call | tf_op jit(solution)/shard_map/focus/pallas_call | solution.py:404
  27.0 0.7 %copy.13 = f32[2,1,1024,16]{2,3,1,0:T(8,128)} copy(f32[2,1,1024,16]{2,3,1,0:T(8,128)S(1)} %bitcast.5) | data formatting | bytes 262144

commit v6 on v5

--- a/solution.py
+++ b/solution.py
@@ -171,23 +171,25 @@
         [(group[k] == 2 * gh + gc).astype(F32) for gh in range(2) for gc in (1 - core, core)] for k in range(NFD)
     ]
     loads[2].wait()
-    for a in range(8):
-        lanes = slice(128 * a, 128 * a + 128)
-        total = [[None, None] for _ in range(4)]
-        for k in range(NFD):
-            c = cosine[k : k + 1, lanes]
-            d = sine[k : k + 1, lanes]
-            re = refl[0, k, :, lanes]
-            im = refl[1, k, :, lanes]
-            turned = (re * c - im * d, re * d + im * c)
-            for g in range(4):
+    def focus(which, target):
+        for a in range(8):
+            lanes = slice(128 * a, 128 * a + 128)
+            total = [[None, None] for _ in range(2)]
+            for k in range(NFD):
+                c = cosine[k : k + 1, lanes]
+                d = sine[k : k + 1, lanes]
+                re = refl[0, k, :, lanes]
+                im = refl[1, k, :, lanes]
+                turned = (re * c - im * d, re * d + im * c)
+                for gh in range(2):
+                    for part in range(2):
+                        term = turned[part] * weights[k][2 * gh + which]
+                        total[gh][part] = term if k == 0 else total[gh][part] + term
+            for gh in range(2):
                 for part in range(2):
-                    term = turned[part] * weights[k][g]
-                    total[g][part] = term if k == 0 else total[g][part] + term
-        for gh in range(2):
-            for part in range(2):
-                core_out[gh, part, :, lanes] = total[2 * gh][part]
-                core_own[gh, part, :, lanes] = total[2 * gh + 1][part]
+                    target[gh, part, :, lanes] = total[gh][part]
+
+    focus(0, core_out)
 
     pl.semaphore_wait(barrier, len(first_peers))
     groups = (1 - y_hi, y_hi)
@@ -202,6 +204,7 @@
         copy.start()
     for peer in x_ring:
         pl.semaphore_signal(plane_sem, inc=1, device_id=peer, device_id_type=MESH)
+    focus(1, core_own)
     loads[3].wait()
     loads[4].wait()
 

time: 27.8 us -> 27.7 us (level)
  no operation moved by 1% of the time
where the time goes in v6:
time: 27.7 us; the launch traced here: 27.6 us
  Pallas kernels  27 us (97%)
  local copies, waits for them, and re-layouts  0.66 us (2%)
    pallas_call x1, Pallas kernels, local(): pl.pallas_call(kernel, out_shape=jax.ShapeDtypeStruct((2, ROWS, N), F32),...  27 us
    unnamed x1, local copies, waits for them, and re-layouts  0.66 us

profile of v6, /device:TPU:226, one launch (start us, length us, event | category | flops | bytes accessed | tf_op | source)
XLA Modules:
  0.0 27.6 jit_solution(12339247629948753523)
XLA Ops:
  0.0 27.0 %focus.1 = f32[2,16,1024]{2,1,0:T(8,128)S(1)} custom-call(f32[2,8,16,1024]{3,2,1,0:T(8,128)} %refl_hbm.1, f32[8,1024]{1,0:T(8,128)} %phase_hbm.1, s32[8]{0:T(128)} %group_hbm.1, s32[1,2]{1,0:T(1,128)} %widths_hbm.1, f32[2,8,128]{2,1,0:T(8,128)} %constant.12.clone.twa_hbm, bf16[2,320,256]{2,1,0:T(8,128)(2,1)} %constant.13.clone.col_hbm, ...), custom_call_target="tpu_custom_call" | custom-call | tf_op jit(solution)/shard_map/focus/pallas_call | solution.py:407
  27.0 0.7 %copy.13 = f32[2,1,1024,16]{2,3,1,0:T(8,128)} copy(f32[2,1,1024,16]{2,3,1,0:T(8,128)S(1)} %bitcast.5) | data formatting | bytes 262144

commit v7 on v6

--- a/solution.py
+++ b/solution.py
@@ -159,7 +159,7 @@
             ]
         )
     ]
-    for load in loads:
+    for load in loads[:3]:
         load.start()
 
     loads[0].wait()
@@ -171,6 +171,8 @@
         [(group[k] == 2 * gh + gc).astype(F32) for gh in range(2) for gc in (1 - core, core)] for k in range(NFD)
     ]
     loads[2].wait()
+    for load in loads[3:]:
+        load.start()
     def focus(which, target):
         for a in range(8):
             lanes = slice(128 * a, 128 * a + 128)

time: 27.7 us -> 27.8 us (level)
  no operation moved by 1% of the time
where the time goes in v7:
time: 27.8 us; the launch traced here: 27.6 us
  Pallas kernels  27 us (97%)
  local copies, waits for them, and re-layouts  0.66 us (2%)
    pallas_call x1, Pallas kernels, local(): pl.pallas_call(kernel, out_shape=jax.ShapeDtypeStruct((2, ROWS, N), F32),...  27 us
    unnamed x1, local copies, waits for them, and re-layouts  0.66 us

profile of v7, /device:TPU:226, one launch (start us, length us, event | category | flops | bytes accessed | tf_op | source)
XLA Modules:
  0.0 27.6 jit_solution(7706644682425296015)
XLA Ops:
  0.0 27.0 %focus.1 = f32[2,16,1024]{2,1,0:T(8,128)S(1)} custom-call(f32[2,8,16,1024]{3,2,1,0:T(8,128)} %refl_hbm.1, f32[8,1024]{1,0:T(8,128)} %phase_hbm.1, s32[8]{0:T(128)} %group_hbm.1, s32[1,2]{1,0:T(1,128)} %widths_hbm.1, f32[2,8,128]{2,1,0:T(8,128)} %constant.12.clone.twa_hbm, bf16[2,320,256]{2,1,0:T(8,128)(2,1)} %constant.13.clone.col_hbm, ...), custom_call_target="tpu_custom_call" | custom-call | tf_op jit(solution)/shard_map/focus/pallas_call | solution.py:409
  27.0 0.7 %copy.13 = f32[2,1,1024,16]{2,3,1,0:T(8,128)} copy(f32[2,1,1024,16]{2,3,1,0:T(8,128)S(1)} %bitcast.5) | data formatting | bytes 262144
